TPU v7x, 128 devices: a whole 4x4x4 slice. The times are simulated.
128 devices in a mesh: row: 8 (over y, z_lo), col: 16 (over z_hi, x, core).
Axes of the slice: x: 4, y: 4, z: 4 (z_hi: 2, z_lo: 2; z = z_hi * 2 + z_lo), core: 2. Of those that a mesh axis runs over, the one named last changes fastest.
Arguments:
- velocities: bfloat16 [1024, 61440], P(None, 'row'), may hold values from -60 to 60, as said below
- modes_panel: bfloat16 [61440, 4096], P('row', 'col'), may hold values from -1 to 1
- atom_slot: int32 [20480], P('row'), may hold values from 0 to 2559, as said below
- lag_offsets: int32 [8], replicated, may hold values from 0 to 256, as said below
Outputs:
- correlations: float32 [8, 4096, 4096], P(None, 'row', 'col')
Inputs may be any that keep to these rules, and one draw needn't show every extreme that they name: `velocities`: every snapshot row has its own scale. Within each aligned block of 2560 atoms, atom_slot is a permutation of 0 to 2559. `lag_offsets`: one of the lags equals 256.
All inputs are finite; a program needn't handle non-finite values.
Results may differ from a plain program's by a relative error of at most 0.0041.
Values may be sent and summed in bfloat16 or wider, within the bound.
A program may use at most 128 MiB of HBM per device.

v0:
```python
import jax
import jax.numpy as jnp
from jax import lax
from jax.sharding import PartitionSpec as P

M = 4096
LAGS = 8
MAXLAG = 256
epsilon = 1e-06


def reorder(modes_panel, atom_slot):
    per_atom = modes_panel.reshape(atom_slot.shape[0], 3, modes_panel.shape[1])
    return jnp.take(per_atom, atom_slot, axis=0).reshape(modes_panel.shape)


def correlate(row_modes, column_modes, lag_offsets):
    snapshots = column_modes.shape[0]
    padded = jnp.concatenate(
        [column_modes, jnp.zeros((MAXLAG, column_modes.shape[1]), jnp.bfloat16)], axis=0
    )
    results = []
    for number in range(LAGS):
        offset = lag_offsets[number]
        shifted = lax.dynamic_slice_in_dim(padded, offset, snapshots, 0)
        product = lax.dot_general(
            row_modes, shifted, (((0,), (0,)), ((), ())), preferred_element_type=jnp.float32
        )
        results.append(product * lax.rsqrt((snapshots - offset).astype(jnp.float32)))
    return jnp.stack(results)


def local(velocities, modes_panel, atom_slot, lag_offsets):
    panel = reorder(modes_panel, atom_slot)
    row_count = lax.axis_size("row")
    partial_terms = jnp.dot(velocities, panel, preferred_element_type=jnp.float32)
    projected = lax.psum(partial_terms, "row")
    energy = lax.psum(jnp.sum(projected * projected, axis=1), "col")
    column_modes = (projected * lax.rsqrt(energy / M + epsilon)[:, None]).astype(jnp.bfloat16)
    block_width = M // row_count
    every_mode = lax.all_gather(column_modes, "col", axis=1, tiled=True)
    row_modes = lax.dynamic_slice_in_dim(
        every_mode, lax.axis_index("row") * block_width, block_width, 1
    )
    return correlate(row_modes, column_modes, lag_offsets)


def solution(mesh):
    return jax.shard_map(
        local,
        mesh=mesh,
        in_specs=(P(None, "row"), P("row", "col"), P("row"), P()),
        out_specs=P(None, "row", "col"),
        check_vma=False,
    )
```

profile of v0, /device:TPU:1, one launch (start us, length us, event | category | flops | bytes accessed | tf_op | source)
XLA Modules:
  0.0 265.8 jit_solution(16931310440080507958)
XLA Ops:
  6.5 0.7 compare_select_fusion
  7.2 0.7 compare_and_fusion
  8.0 11.0 %reshape.12 = bf16[2560,3,256]{2,1,0:T(4,128)(2,1)} reshape(bf16[7680,256]{1,0:T(8,128)(2,1)} %param.5) | data formatting | bytes 7864320 | tf_op jit(solution)/shard_map/reshape | solution.py:13
  18.9 13.3 %gather_fusion = bf16[2560,3,256]{2,1,0:T(4,128)(2,1)} fusion(bf16[2560,3,256]{2,1,0:T(4,128)(2,1)} %reshape.12, s32[3072]{0:T(1024)S(1)} %pad_clamp_fusion), kind=kCustom, calls=%fused_computation | custom fusion | bytes 7874560 | tf_op jit(solution)/shard_map/jit(_take)/gather | solution.py:14
  32.3 10.7 %gather.7 = bf16[7680,256]{1,0:T(8,128)(2,1)} reshape(bf16[2560,3,256]{2,1,0:T(4,128)(2,1)} %gather_fusion) | data formatting | bytes 7864320 | tf_op jit(solution)/shard_map/jit(_take)/gather | solution.py:14
  42.9 1.3 broadcast_in_dim.18
  44.3 1.1 broadcast_in_dim.19
  45.3 12.0 %fusion.4 = f32[1024,256]{0,1:T(8,128)} fusion(bf16[1024,7680]{1,0:T(8,128)(2,1)} %param.4, bf16[7680,256]{1,0:T(8,128)(2,1)} %gather.7, pred[7680]{0:T(1024)(128)(4,1)S(1)} %broadcast_in_dim.19), kind=kOutput, calls=%fused_computation.5 | convolution fusion | flops 4028497920 | bytes 20717056 | tf_op jit(solution)/shard_map/dot_general | solution.py:36
  57.3 0.0 all-gather.2.cloned.1.call-start
  57.4 77.0 %all-reduce.3.cloned.1.call-done = f32[1024,256]{0,1:T(8,128)} async-done(((f32[1024,256]{0,1:T(8,128)}), f32[1024,256]{0,1:T(8,128)}) %all-reduce.3.cloned.1.call-update) | async-done | bytes 1048592 | tf_op jit(solution)/shard_map/psum | solution.py:37
  134.4 1.3 multiply_reduce_fusion
  135.7 37.5 %psum.15 = f32[1024]{0:T(1024)S(1)} all-reduce(f32[1024]{0:T(1024)S(1)} %multiply_reduce_fusion), channel_id=1, replica_groups=mesh['row'=8,'col'=16] {'col'}, use_global_device_ids=true, to_apply=%region_2.3 | all-reduce | flops 1024 | bytes 8192 | tf_op jit(solution)/shard_map/psum | solution.py:38
  173.2 2.1 multiply_convert_fusion
  175.4 0.7 fusion.48
  196.7 49.1 %all-gather.2.cloned.1.call-done = bf16[1024,4096]{0,1:T(8,128)(2,1)} async-done(((bf16[1024,256]{0,1:T(8,128)(2,1)}), bf16[1024,4096]{0,1:T(8,128)(2,1)}) %all-gather.2.cloned.1.call-update) | async-done | bytes 8388624 | tf_op jit(solution)/shard_map/all_gather | solution.py:41
  245.8 2.0 fusion.22
  247.9 2.4 fusion.20
  250.3 1.8 fusion.18
  252.1 1.8 fusion.16
  253.9 0.6 fusion.14
  254.4 0.6 fusion.12
  255.0 0.6 fusion.10
  255.6 2.0 copy-done.3
  257.6 1.4 fusion.8
  (12 shorter events, 0.1 us)
Async XLA Ops:
  6.5 127.8 %all-reduce.3.cloned.1.call-start = ((), (), s32[]{:S(2)}) async-start(), calls=%async_computation | async-start | bytes 2097152 | tf_op jit(solution)/shard_map/psum | solution.py:37
  57.3 118.1 %copy-start.1 = (s32[8]{0:T(128)S(1)}, s32[8]{0:T(128)}, u32[]{:S(2)}) copy-start(s32[8]{0:T(128)} %param.7) | copy-start | bytes 100
  57.3 188.5 %all-gather.2.cloned.1.call-start = ((), (), s32[]{:S(2)}) async-start(), calls=%async_computation.1 | async-start | bytes 8912896 | tf_op jit(solution)/shard_map/all_gather | solution.py:41
  175.3 74.9 %copy-start = (bf16[1024,256]{0,1:T(8,128)(2,1)S(1)}, bf16[1024,256]{0,1:T(8,128)(2,1)}, u32[]{:S(2)}) copy-start(bf16[1024,256]{0,1:T(8,128)(2,1)} %multiply_convert_fusion) | copy-start | bytes 1572868
  245.8 8.0 %copy-start.2 = (bf16[1024,4096]{0,1:T(8,128)(2,1)S(1)}, bf16[1024,4096]{0,1:T(8,128)(2,1)}, u32[]{:S(2)}) copy-start(bf16[1024,4096]{0,1:T(8,128)(2,1)} %all-gather.2.cloned.1.call-done) | copy-start | bytes 25165828
  255.6 2.0 copy-start.3
Sparse Core Ops, SparseCore 0:
  57.5 76.8 all-reduce.2
  175.5 70.2 all-gather.1
where the time goes:
time: 267 us; the launch traced here: 266 us
  waiting for transfers between devices  126 us (47%)
  local copies, waits for them, and re-layouts  40.1 us (15%)
  blocking collectives  37.5 us (14%)
  between operations  34.2 us (13%)
  matrix products  23 us (9%)
  other arithmetic  4.87 us (2%)
    psum x1, waiting for transfers between devices, local(): projected = lax.psum(partial_terms, 'row')  77 us
    all_gather x1, waiting for transfers between devices, local(): every_mode = lax.all_gather(column_modes, 'col', axis=1, tiled=True)  49.1 us
    psum x1, blocking collectives, local(): energy = lax.psum(jnp.sum(projected * projected, axis=1), 'col')  37.5 us
    gather x2, local copies, waits for them, and re-layouts, reorder(): return jnp.take(per_atom, atom_slot, axis=0).reshape(modes_panel.shape)  24 us
    dot_general x1, matrix products, local(): jnp.dot(velocities, panel, preferred_element_type=jnp.float32)  12 us
    dot_general x8, matrix products, correlate(): lax.dot_general(row_modes, shifted, (((0,), (0,)), ((), ())), preferred_e...  11.1 us
    reshape x1, local copies, waits for them, and re-layouts, reorder(): per_atom = modes_panel.reshape(atom_slot.shape[0], 3, modes_panel.shape[1])  11 us
  transfers between devices with their start and end apart: 2, of which 2 were waited for; matrix products, arithmetic and copies ran while one was open for 0% of the time, Pallas kernels for 0%

commit v1 on v0

--- a/solution.py
+++ b/solution.py
@@ -7,6 +7,12 @@
 LAGS = 8
 MAXLAG = 256
 epsilon = 1e-06
+
+
+def bands_end(target):
+    return jnp.concatenate(
+        lax.all_to_all(jnp.stack(lax.axis_size("col") * [target], axis=0), "col", 0, 0), axis=1
+    )
 
 
 def reorder(modes_panel, atom_slot):
@@ -38,7 +44,7 @@
     energy = lax.psum(jnp.sum(projected * projected, axis=1), "col")
     column_modes = (projected * lax.rsqrt(energy / M + epsilon)[:, None]).astype(jnp.bfloat16)
     block_width = M // row_count
-    every_mode = lax.all_gather(column_modes, "col", axis=1, tiled=True)
+    every_mode = bands_end(column_modes)
     row_modes = lax.dynamic_slice_in_dim(
         every_mode, lax.axis_index("row") * block_width, block_width, 1
     )

time: 267 us -> 322 us (1.21)
  waiting for transfers between devices: 126 us -> 168 us
  starting transfers between devices: 0.04 us -> 5.25 us
  local copies, waits for them, and re-layouts: 40.1 us -> 44.3 us
  matrix products: 23 us -> 27.1 us
    all_to_all x0 -> x1, waiting for transfers between devices: none -> 90.9 us  [bands_end(): lax.all_to_all(jnp.stack(lax.axis_size('col') * [target], axis=0), 'col',...]
    all_gather x1 -> x0, waiting for transfers between devices: 49.1 us -> none  [local(): every_mode = lax.all_gather(column_modes, 'col', axis=1, tiled=True)]
    all_to_all x0 -> x1, starting transfers between devices: none -> 5.24 us  [bands_end(): lax.all_to_all(jnp.stack(lax.axis_size('col') * [target], axis=0), 'col',...]
    another operation x0 -> x1, local copies, waits for them, and re-layouts: none -> 4.29 us  [bands_end(): jnp.stack(lax.axis_size('col') * [target], axis=0)]
    dot_general x8, matrix products: 11.1 us -> 15.1 us  [correlate(): lax.dot_general(row_modes, shifted, (((0,), (0,)), ((), ())), preferred_e...]
where the time goes in v1:
time: 322 us; the launch traced here: 320 us
  waiting for transfers between devices  168 us (52%)
  local copies, waits for them, and re-layouts  44.3 us (14%)
  blocking collectives  37.3 us (12%)
  between operations  34 us (11%)
  matrix products  27.1 us (8%)
  starting transfers between devices  5.25 us (2%)
  other arithmetic  4.08 us (1%)
    all_to_all x1, waiting for transfers between devices, bands_end(): lax.all_to_all(jnp.stack(lax.axis_size('col') * [target], axis=0), 'col',...  90.9 us
    psum x1, waiting for transfers between devices, local(): projected = lax.psum(partial_terms, 'row')  77.2 us
    psum x1, blocking collectives, local(): energy = lax.psum(jnp.sum(projected * projected, axis=1), 'col')  37.3 us
    gather x2, local copies, waits for them, and re-layouts, reorder(): return jnp.take(per_atom, atom_slot, axis=0).reshape(modes_panel.shape)  24 us
    dot_general x8, matrix products, correlate(): lax.dot_general(row_modes, shifted, (((0,), (0,)), ((), ())), preferred_e...  15.1 us
    dot_general x1, matrix products, local(): jnp.dot(velocities, panel, preferred_element_type=jnp.float32)  12 us
    reshape x1, local copies, waits for them, and re-layouts, reorder(): per_atom = modes_panel.reshape(atom_slot.shape[0], 3, modes_panel.shape[1])  11 us
  transfers between devices with their start and end apart: 2, of which 2 were waited for; matrix products, arithmetic and copies ran while one was open for 0% of the time, Pallas kernels for 0%

profile of v1, /device:TPU:1, one launch (start us, length us, event | category | flops | bytes accessed | tf_op | source)
XLA Modules:
  0.0 320.3 jit_solution(14458628609356651888)
XLA Ops:
  6.5 0.7 compare_select_fusion
  7.2 0.7 compare_and_fusion
  8.0 11.0 %reshape.20 = bf16[2560,3,256]{2,1,0:T(4,128)(2,1)} reshape(bf16[7680,256]{1,0:T(8,128)(2,1)} %param.5) | data formatting | bytes 7864320 | tf_op jit(solution)/shard_map/reshape | solution.py:19
  18.9 13.3 %gather_fusion = bf16[2560,3,256]{2,1,0:T(4,128)(2,1)} fusion(bf16[2560,3,256]{2,1,0:T(4,128)(2,1)} %reshape.20, s32[3072]{0:T(1024)S(1)} %pad_clamp_fusion), kind=kCustom, calls=%fused_computation | custom fusion | bytes 7874560 | tf_op jit(solution)/shard_map/jit(_take)/gather | solution.py:20
  32.3 10.7 %gather.7 = bf16[7680,256]{1,0:T(8,128)(2,1)} reshape(bf16[2560,3,256]{2,1,0:T(4,128)(2,1)} %gather_fusion) | data formatting | bytes 7864320 | tf_op jit(solution)/shard_map/jit(_take)/gather | solution.py:20
  42.9 1.3 broadcast_in_dim.18
  44.3 1.1 broadcast_in_dim.19
  45.3 12.0 %fusion.4 = f32[1024,256]{0,1:T(8,128)} fusion(bf16[1024,7680]{1,0:T(8,128)(2,1)} %param.4, bf16[7680,256]{1,0:T(8,128)(2,1)} %gather.7, pred[7680]{0:T(1024)(128)(4,1)S(1)} %broadcast_in_dim.19), kind=kOutput, calls=%fused_computation.5 | convolution fusion | flops 4028497920 | bytes 20717056 | tf_op jit(solution)/shard_map/dot_general | solution.py:42
  57.3 77.2 %all-reduce.3.cloned.1.call-done = f32[1024,256]{0,1:T(8,128)} async-done(((f32[1024,256]{0,1:T(8,128)}), f32[1024,256]{0,1:T(8,128)}) %all-reduce.3.cloned.1.call-update) | async-done | bytes 1048592 | tf_op jit(solution)/shard_map/psum | solution.py:43
  134.5 1.3 multiply_reduce_fusion
  135.9 37.3 %psum.15 = f32[1024]{0:T(1024)S(1)} all-reduce(f32[1024]{0:T(1024)S(1)} %multiply_reduce_fusion), channel_id=1, replica_groups=mesh['row'=8,'col'=16] {'col'}, use_global_device_ids=true, to_apply=%region_2.3 | all-reduce | flops 1024 | bytes 8192 | tf_op jit(solution)/shard_map/psum | solution.py:44
  173.2 1.3 multiply_convert_fusion
  174.5 4.3 %stack.20 = bf16[16,1024,256]{1,2,0:T(8,128)(2,1)} broadcast(bf16[1024,256]{0,1:T(8,128)(2,1)S(1)} %multiply_convert_fusion), dimensions={1,2} | broadcast | bytes 8912896 | tf_op jit(solution)/shard_map/stack | solution.py:14
  178.8 5.2 %all-to-all-start = ((bf16[16,1024,256]{1,2,0:T(8,128)(2,1)}), bf16[16,1024,256]{1,2,0:T(8,128)(2,1)}, u32[]{:S(2)}, u32[]{:S(2)}) async-start(bf16[16,1024,256]{1,2,0:T(8,128)(2,1)} %stack.20), calls=%async_computation | async-start | bytes 16777216 | tf_op jit(solution)/shard_map/all_to_all | solution.py:14
  205.3 90.9 %all-to-all-done = bf16[16,1024,256]{1,2,0:T(8,128)(2,1)} async-done(((bf16[16,1024,256]{1,2,0:T(8,128)(2,1)}), bf16[16,1024,256]{1,2,0:T(8,128)(2,1)}, u32[]{:S(2)}, u32[]{:S(2)}) %all-to-all-start) | async-done | bytes 8388640 | tf_op jit(solution)/shard_map/all_to_all | solution.py:14
  296.2 1.8 fusion.22
  298.0 1.8 fusion.20
  299.8 1.8 fusion.18
  301.6 1.8 fusion.16
  303.4 1.8 fusion.14
  305.2 1.8 fusion.12
  307.0 1.8 fusion.10
  308.8 2.0 copy-done.1
  310.8 2.6 fusion.8
  (8 shorter events, 0.7 us)
Async XLA Ops:
  6.5 128.0 %all-reduce.3.cloned.1.call-start = ((), (), s32[]{:S(2)}) async-start(), calls=%async_computation.1 | async-start | bytes 2097152 | tf_op jit(solution)/shard_map/psum | solution.py:43
  178.8 5.2 %copy-start = (s32[8]{0:T(128)S(1)}, s32[8]{0:T(128)}, u32[]{:S(2)}) copy-start(s32[8]{0:T(128)} %param.7) | copy-start | bytes 100
  178.8 117.4 %all-to-all-start = ((bf16[16,1024,256]{1,2,0:T(8,128)(2,1)}), bf16[16,1024,256]{1,2,0:T(8,128)(2,1)}, u32[]{:S(2)}, u32[]{:S(2)}) async-start(bf16[16,1024,256]{1,2,0:T(8,128)(2,1)} %stack.20), calls=%async_computation | async-start | bytes 16777216 | tf_op jit(solution)/shard_map/all_to_all | solution.py:14
  308.8 2.0 copy-start.1
Sparse Core Ops, SparseCore 0:
  57.5 77.0 all-reduce.2
